TPU v7x, 1024 devices: a whole 4x4x32 slice. The times are simulated.
1024 devices in a mesh: dp: 64 (over z, core), expert: 16 (over y, x).
Axes of the slice: x: 4, y: 4, z: 32, core: 2. Of those that a mesh axis runs over, the one named last changes fastest.
Arguments:
- grads: bfloat16 [16, 64, 1024, 768], P('expert', 'dp'), may hold values from -3000 to 3000
- momentum: float32 [64, 1024, 768], P('dp', 'expert'), may hold values from -3000 to 3000
Outputs:
- update: bfloat16 [64, 1024, 768], P('dp', 'expert')
- new_momentum: float32 [64, 1024, 768], P('dp', 'expert')
All inputs are finite; a program needn't handle non-finite values.
Results may differ from a plain program's by a relative error of at most 0.023.
Values may be sent and summed in bfloat16 or wider, within the bound.
No kernel may reach another device: no remote copies, remote signals or barrier semaphores. Data moves between devices by JAX's collectives and lax.ppermute only.
A program may use at most 32 MiB of HBM per device.

v0:
```python
import math

import jax
import jax.numpy as jnp
from jax import lax
from jax.sharding import PartitionSpec as P

D = 1024
R = 768
ITERS = 3


rate = 0.95
eps = 1e-07
coef_a = 3.4445
coef_b = -4.775
coef_c = 2.0315
batch_dims = ((0,), (0,))


def shards(grads, momentum):
    terms = grads[0].astype(jnp.float32)
    total = lax.psum_scatter(
        terms.astype(jnp.bfloat16), "expert", scatter_dimension=1, tiled=True
    ).astype(jnp.float32)
    new_momentum = rate * momentum + total
    blend = total + rate * new_momentum
    squares = lax.psum(jnp.sum(blend * blend, axis=(1, 2)), "expert")
    iterate = (blend / (jnp.sqrt(squares)[:, None, None] + eps)).astype(jnp.bfloat16)
    for step in range(ITERS):
        partial_gram = lax.dot_general(
            iterate, iterate, (((1,), (1,)), batch_dims), preferred_element_type=jnp.float32
        )
        share = lax.psum_scatter(
            partial_gram.astype(jnp.bfloat16), "expert", scatter_dimension=1, tiled=True
        )
        gram = lax.all_gather(share, "expert", axis=1, tiled=True)
        square = lax.dot_general(
            gram, gram, (((2,), (1,)), batch_dims), preferred_element_type=jnp.float32
        )
        poly = (coef_b * gram.astype(jnp.float32) + coef_c * square).astype(jnp.bfloat16)
        product = lax.dot_general(
            iterate, poly, (((2,), (1,)), batch_dims), preferred_element_type=jnp.float32
        )
        iterate = (coef_a * iterate.astype(jnp.float32) + product).astype(jnp.bfloat16)
    factor = 0.2 * math.sqrt(max(D, R))
    update = (factor * iterate.astype(jnp.float32)).astype(jnp.bfloat16)
    return (update, new_momentum)


def solution(mesh):
    return jax.shard_map(
        shards,
        mesh=mesh,
        in_specs=(P("expert", "dp", None, None), P("dp", "expert", None)),
        out_specs=(P("dp", "expert", None), P("dp", "expert", None)),
        check_vma=False,
    )
```

profile of v0, /device:TPU:992, one launch (start us, length us, event | category | flops | bytes accessed | tf_op | source)
XLA Modules:
  0.0 755.7 jit_solution(3473971635513480279)
XLA Ops:
  7.2 0.0 copy-start.1
  7.2 0.0 reduce-scatter.5.cloned.1.call-start
  7.2 0.7 reduce-scatter.5.cloned.1.call-update
  7.9 0.0 reduce-scatter.7.cloned.1.call-start
  8.0 111.0 %reduce-scatter.5.cloned.1.call-done = bf16[1,64,768]{2,1,0:T(8,128)(2,1)} async-done(((bf16[1,1024,768]{2,1,0:T(8,128)(2,1)}), bf16[1,64,768]{2,1,0:T(8,128)(2,1)}) %reduce-scatter.5.cloned.1.call-update) | async-done | bytes 98320 | tf_op jit(solution)/shard_map/reduce_scatter | solution.py:23
  118.9 0.0 copy-done.1
  118.9 1.6 multiply_reduce_fusion
  120.5 38.7 %psum.7 = f32[1]{0:T(128)} all-reduce(f32[1]{0:T(128)} %bitcast.1), channel_id=1, replica_groups=mesh['dp'=64,'expert'=16] {'expert'}, use_global_device_ids=true, to_apply=%region_2.0 | all-reduce | flops 1 | bytes 8 | tf_op jit(solution)/shard_map/psum | solution.py:28
  159.9 0.9 divide_convert_fusion
  160.8 1.5 fusion.3
  162.4 0.0 reduce-scatter.7.cloned.1.call-update
  162.4 0.0 all-gather.4.cloned.1.call-start
  162.4 105.8 %reduce-scatter.7.cloned.1.call-done = bf16[1,48,768]{2,1,0:T(8,128)(2,1)} async-done(((bf16[1,768,768]{2,1,0:T(8,128)(2,1)}), bf16[1,48,768]{2,1,0:T(8,128)(2,1)}) %reduce-scatter.7.cloned.1.call-update) | async-done | bytes 73744 | tf_op jit(solution)/shard_map/reduce_scatter | solution.py:34
  268.3 0.0 all-gather.4.cloned.1.call-update
  268.3 0.0 reduce-scatter.9.cloned.1.call-start
  268.3 82.7 %all-gather.4.cloned.1.call-done = bf16[1,768,768]{2,1,0:T(8,128)(2,1)} async-done(((bf16[1,48,768]{2,1,0:T(8,128)(2,1)}), bf16[1,768,768]{2,1,0:T(8,128)(2,1)}) %all-gather.4.cloned.1.call-update) | async-done | bytes 1179664 | tf_op jit(solution)/shard_map/all_gather | solution.py:37
  351.1 3.7 fusion.42
  354.8 1.5 fusion.4
  356.3 0.0 reduce-scatter.9.cloned.1.call-update
  356.3 0.0 all-gather.6.cloned.1.call-start
  356.4 108.7 %reduce-scatter.9.cloned.1.call-done = bf16[1,48,768]{2,1,0:T(8,128)(2,1)} async-done(((bf16[1,768,768]{2,1,0:T(8,128)(2,1)}), bf16[1,48,768]{2,1,0:T(8,128)(2,1)}) %reduce-scatter.9.cloned.1.call-update) | async-done | bytes 73744 | tf_op jit(solution)/shard_map/reduce_scatter | solution.py:34
  465.1 0.0 all-gather.6.cloned.1.call-update
  465.1 0.0 reduce-scatter.11.cloned.1.call-start
  465.2 82.5 %all-gather.6.cloned.1.call-done = bf16[1,768,768]{2,1,0:T(8,128)(2,1)} async-done(((bf16[1,48,768]{2,1,0:T(8,128)(2,1)}), bf16[1,768,768]{2,1,0:T(8,128)(2,1)}) %all-gather.6.cloned.1.call-update) | async-done | bytes 1179664 | tf_op jit(solution)/shard_map/all_gather | solution.py:37
  547.7 3.7 fusion.45
  551.4 1.5 fusion.5
  552.9 0.0 reduce-scatter.11.cloned.1.call-update
  553.0 0.0 all-gather.8.cloned.1.call-start
  553.0 108.7 %reduce-scatter.11.cloned.1.call-done = bf16[1,48,768]{2,1,0:T(8,128)(2,1)} async-done(((bf16[1,768,768]{2,1,0:T(8,128)(2,1)}), bf16[1,48,768]{2,1,0:T(8,128)(2,1)}) %reduce-scatter.11.cloned.1.call-update) | async-done | bytes 73744 | tf_op jit(solution)/shard_map/reduce_scatter | solution.py:34
  661.8 0.0 all-gather.8.cloned.1.call-update
  661.8 82.7 %all-gather.8.cloned.1.call-done = bf16[1,768,768]{2,1,0:T(8,128)(2,1)} async-done(((bf16[1,48,768]{2,1,0:T(8,128)(2,1)}), bf16[1,768,768]{2,1,0:T(8,128)(2,1)}) %all-gather.8.cloned.1.call-update) | async-done | bytes 1179664 | tf_op jit(solution)/shard_map/all_gather | solution.py:37
  744.5 4.3 fusion.57
  (2 shorter events, 0.0 us)
Async XLA Ops:
  7.2 111.8 %copy-start.1 = (f32[1,64,768]{2,1,0:T(8,128)S(1)}, f32[1,64,768]{2,1,0:T(8,128)}, u32[]{:S(2)}) copy-start(f32[1,64,768]{2,1,0:T(8,128)} %param.3) | copy-start | bytes 589828
  7.2 111.8 %reduce-scatter.5.cloned.1.call-start = ((), (), s32[]{:S(2)}) async-start(), calls=%async_computation.4 | async-start | bytes 1671168 | tf_op jit(solution)/shard_map/reduce_scatter | solution.py:23
  7.9 260.4 %reduce-scatter.7.cloned.1.call-start = ((), (), s32[]{:S(2)}) async-start(), calls=%async_computation.5 | async-start | bytes 1253376 | tf_op jit(solution)/shard_map/reduce_scatter | solution.py:34
  120.5 41.9 %copy-start = (f32[1,64,768]{2,1,0:T(8,128)}, f32[1,64,768]{2,1,0:T(8,128)S(1)}, u32[]{:S(2)}) copy-start(f32[1,64,768]{2,1,0:T(8,128)S(1)} %get-tuple-element.3) | copy-start | bytes 589828
  162.4 188.7 %all-gather.4.cloned.1.call-start = ((), (), s32[]{:S(2)}) async-start(), calls=%async_computation.6 | async-start | bytes 1253376 | tf_op jit(solution)/shard_map/all_gather | solution.py:37
  268.3 196.8 %reduce-scatter.9.cloned.1.call-start = ((), (), s32[]{:S(2)}) async-start(), calls=%async_computation.7 | async-start | bytes 1253376 | tf_op jit(solution)/shard_map/reduce_scatter | solution.py:34
  356.3 191.4 %all-gather.6.cloned.1.call-start = ((), (), s32[]{:S(2)}) async-start(), calls=%async_computation.8 | async-start | bytes 1253376 | tf_op jit(solution)/shard_map/all_gather | solution.py:37
  465.1 196.6 %reduce-scatter.11.cloned.1.call-start = ((), (), s32[]{:S(2)}) async-start(), calls=%async_computation.9 | async-start | bytes 1253376 | tf_op jit(solution)/shard_map/reduce_scatter | solution.py:34
  553.0 191.6 %all-gather.8.cloned.1.call-start = ((), (), s32[]{:S(2)}) async-start(), calls=%async_computation.10 | async-start | bytes 1253376 | tf_op jit(solution)/shard_map/all_gather | solution.py:37
Sparse Core Ops, SparseCore 0:
  13.3 105.6 reduce-scatter.4
  162.5 105.7 reduce-scatter.6
  272.4 78.5 all-gather.3
  356.4 108.6 reduce-scatter.8
  469.1 78.5 all-gather.5
  553.1 108.6 reduce-scatter.10
  665.9 78.5 all-gather.7
where the time goes:
time: 767 us; the launch traced here: 756 us
  waiting for transfers between devices  683 us (89%)
  blocking collectives  38.7 us (5%)
  matrix products  16.3 us (2%)
  between operations  14.9 us (2%)
    reduce_scatter x3, waiting for transfers between devices, shards(): lax.psum_scatter(partial_gram.astype(jnp.bfloat16), 'expert', scatter_dim...  323 us
    all_gather x3, waiting for transfers between devices, shards(): gram = lax.all_gather(share, 'expert', axis=1, tiled=True)  248 us
    reduce_scatter x1, waiting for transfers between devices, shards(): lax.psum_scatter(terms.astype(jnp.bfloat16), 'expert', scatter_dimension=...  111 us
    psum x1, blocking collectives, shards(): squares = lax.psum(jnp.sum(blend * blend, axis=(1, 2)), 'expert')  38.7 us
  transfers between devices with their start and end apart: 7, of which 7 were waited for; matrix products, arithmetic and copies ran while one was open for 0% of the time, Pallas kernels for 0%

commit v1 on v0

v1 whole, which is shorter than its diff:
```python
import functools
import math

import jax
import jax.numpy as jnp
from jax import lax
from jax.experimental import pallas as pl
from jax.experimental.pallas import tpu as pltpu
from jax.sharding import PartitionSpec as P

D = 1024
R = 768
ITERS = 3
N_EXPERT = 16
ROWS = D // N_EXPERT


rate = 0.95
eps = 1e-07
coef_a = 3.4445
coef_b = -4.775
coef_c = 2.0315
f32 = jnp.float32
bf16 = jnp.bfloat16


def dot(lhs, rhs, side=1):
    return lax.dot_general(lhs, rhs, (((side,), (0,)), ((), ())), preferred_element_type=f32)


def newton_schulz(whole_ref, own_ref, out_ref, wide, gram, poly, half, rows):
    wide[...] = dot(whole_ref[...], whole_ref[...], side=0)
    diagonal = lax.broadcasted_iota(jnp.int32, (R, R), 0) == lax.broadcasted_iota(jnp.int32, (R, R), 1)
    squares = jnp.full((1, 1), jnp.sum(jnp.where(diagonal, wide[...], 0.0)), f32)
    inverse = 1.0 / (jnp.sqrt(squares) + eps)
    gram[...] = (wide[...] * inverse * inverse).astype(bf16)
    rows[...] = own_ref[...]
    for step in range(ITERS):
        square = dot(gram[...], gram[...])
        poly[...] = (coef_b * gram[...].astype(f32) + coef_c * square).astype(bf16)
        if step < ITERS - 1:
            half[...] = (coef_a * gram[...].astype(f32) + dot(gram[...], poly[...])).astype(bf16)
            gram[...] = (coef_a * half[...].astype(f32) + dot(half[...], poly[...])).astype(bf16)
        moved = coef_a * rows[...].astype(f32) + dot(rows[...], poly[...])
        if step == 0:
            moved = moved * inverse
        rows[...] = moved.astype(bf16)
    factor = 0.2 * math.sqrt(max(D, R))
    out_ref[...] = (factor * rows[...].astype(f32)).astype(bf16)


def orthogonalize(whole, own):
    vmem = pl.BlockSpec(memory_space=pltpu.VMEM)
    return pl.pallas_call(
        newton_schulz,
        out_shape=jax.ShapeDtypeStruct((ROWS, R), bf16),
        in_specs=[vmem, vmem],
        out_specs=vmem,
        scratch_shapes=[
            pltpu.VMEM((R, R), f32),
            pltpu.VMEM((R, R), bf16),
            pltpu.VMEM((R, R), bf16),
            pltpu.VMEM((R, R), bf16),
            pltpu.VMEM((ROWS, R), bf16),
        ],
        compiler_params=pltpu.CompilerParams(vmem_limit_bytes=40 * 2**20),
    )(whole, own)


def exchange(blocks):
    return lax.all_to_all(blocks, "expert", 0, 0, tiled=True)


def shards(grads, momentum):
    terms = exchange(grads.reshape(N_EXPERT, ROWS, R))
    total = jnp.sum(terms.astype(f32), axis=0)
    new_momentum = rate * momentum[0] + total
    blend = (total + rate * new_momentum).astype(bf16)
    whole = exchange(jnp.broadcast_to(blend[None], (N_EXPERT, ROWS, R))).reshape(D, R)
    update = orthogonalize(whole, blend)
    return (update[None], new_momentum[None])


def solution(mesh):
    return jax.shard_map(
        shards,
        mesh=mesh,
        in_specs=(P("expert", "dp", None, None), P("dp", "expert", None)),
        out_specs=(P("dp", "expert", None), P("dp", "expert", None)),
        check_vma=False,
    )
```

time: 767 us -> 70.2 us (0.09); the launches traced: 756 us -> 69.9 us
  waiting for transfers between devices: 683 us -> 22.4 us
  matrix products: 16.3 us -> 0 us
  between operations: 14.9 us -> 0.65 us
  Pallas kernels: 0 us -> 10.3 us
  blocking collectives: 38.7 us -> 29.8 us
    reduce_scatter x4 -> x0, waiting for transfers between devices: 434 us -> none  [the longest x3 323 us: shards(): lax.psum_scatter(partial_gram.astype(jnp.bfloat16), 'expert', scatter_dim...]
    all_gather x3 -> x0, waiting for transfers between devices: 248 us -> none  [shards(): gram = lax.all_gather(share, 'expert', axis=1, tiled=True)]
    psum x1 -> x0, blocking collectives: 38.7 us -> none  [shards(): squares = lax.psum(jnp.sum(blend * blend, axis=(1, 2)), 'expert')]
    all_to_all x0 -> x1, blocking collectives: none -> 29.8 us  [exchange(): return lax.all_to_all(blocks, 'expert', 0, 0, tiled=True)]
    all_to_all x0 -> x1, waiting for transfers between devices: none -> 22.4 us  [exchange(): return lax.all_to_all(blocks, 'expert', 0, 0, tiled=True)]
    dot_general x6 -> x0, matrix products: 16.3 us -> none  [the longest x3 11.7 us: shards(): lax.dot_general(iterate, poly, (((2,), (1,)), batch_dims), preferred_elem...]
    pallas_call x0 -> x1, Pallas kernels: none -> 10.3 us  [orthogonalize(): pl.pallas_call(newton_schulz, out_shape=jax.ShapeDtypeStruct((ROWS, R), b...]
  transfers between devices with their start and end apart: 7 -> 1, of which waited for: 7 -> 1; matrix products, arithmetic and copies ran while one was open for 0% -> 0% of each run, Pallas kernels for 0% -> 0%
where the time goes in v1:
time: 70.2 us; the launch traced here: 69.9 us
  blocking collectives  29.8 us (42%)
  waiting for transfers between devices  22.4 us (32%)
  Pallas kernels  10.3 us (15%)
  starting transfers between devices  3.71 us (5%)
  local copies, waits for them, and re-layouts  2.02 us (3%)
  other arithmetic  0.96 us (1%)
    all_to_all x1, blocking collectives, exchange(): return lax.all_to_all(blocks, 'expert', 0, 0, tiled=True)  29.8 us
    all_to_all x1, waiting for transfers between devices, exchange(): return lax.all_to_all(blocks, 'expert', 0, 0, tiled=True)  22.4 us
    pallas_call x1, Pallas kernels, orthogonalize(): pl.pallas_call(newton_schulz, out_shape=jax.ShapeDtypeStruct((ROWS, R), b...  10.3 us
    all_to_all x1, starting transfers between devices, exchange(): return lax.all_to_all(blocks, 'expert', 0, 0, tiled=True)  3.71 us
  transfers between devices with their start and end apart: 1, of which 1 were waited for; matrix products, arithmetic and copies ran while one was open for 0% of the time, Pallas kernels for 0%

profile of v1, /device:TPU:992, one launch (start us, length us, event | category | flops | bytes accessed | tf_op | source)
XLA Modules:
  0.0 69.9 jit_solution(7119255409585259636)
XLA Ops:
  0.6 29.8 %all_to_all.10 = bf16[16,64,768]{2,1,0:T(8,128)(2,1)S(1)} all-to-all(bf16[16,64,768]{2,1,0:T(8,128)(2,1)} %bitcast.22), channel_id=1, replica_groups=mesh['dp'=64,'expert'=16] {'expert'}, dimensions={0} | all-to-all | bytes 3145728 | tf_op jit(solution)/shard_map/all_to_all | solution.py:71
  30.4 0.0 copy-start
  30.4 0.2 convert_reduce_fusion
  30.7 0.7 %copy-done = f32[1,64,768]{2,1,0:T(8,128)S(1)} copy-done((f32[1,64,768]{2,1,0:T(8,128)S(1)}, f32[1,64,768]{2,1,0:T(8,128)}, u32[]{:S(2)}) %copy-start) | copy-done | bytes 196632
  31.4 0.7 %fusion.4 = (bf16[64,768]{1,0:T(8,128)(2,1)S(1)}, f32[1,64,768]{2,1,0:T(8,128)}) fusion(f32[64,768]{1,0:T(8,128)S(1)} %convert_reduce_fusion, f32[1,64,768]{2,1,0:T(8,128)S(1)} %copy-done), kind=kLoop, calls=%fused_computation.8 | loop fusion | flops 245760 | bytes 688128 | tf_op jit(solution)/shard_map/broadcast_in_dim | solution.py:79
  32.1 1.3 %broadcast_in_dim.13 = bf16[16,64,768]{2,1,0:T(8,128)(2,1)} broadcast(bf16[64,768]{1,0:T(8,128)(2,1)S(1)} %get-tuple-element.2), dimensions={1,2} | broadcast | bytes 1671168 | tf_op jit(solution)/shard_map/broadcast_in_dim | solution.py:79
  33.4 3.7 %all-to-all-start.1 = ((bf16[16,64,768]{2,1,0:T(8,128)(2,1)}), bf16[16,64,768]{2,1,0:T(8,128)(2,1)S(1)}, u32[]{:S(2)}, u32[]{:S(2)}) async-start(bf16[16,64,768]{2,1,0:T(8,128)(2,1)} %broadcast_in_dim.13), calls=%async_computation.1 | async-start | bytes 3145728 | tf_op jit(solution)/shard_map/all_to_all | solution.py:71
  37.2 22.4 %all-to-all-done.1 = bf16[16,64,768]{2,1,0:T(8,128)(2,1)S(1)} async-done(((bf16[16,64,768]{2,1,0:T(8,128)(2,1)}), bf16[16,64,768]{2,1,0:T(8,128)(2,1)S(1)}, u32[]{:S(2)}, u32[]{:S(2)}) %all-to-all-start.1) | async-done | bytes 1572896 | tf_op jit(solution)/shard_map/all_to_all | solution.py:71
  59.6 10.3 %shard_map.41 = bf16[64,768]{1,0:T(8,128)(2,1)} custom-call(bf16[1024,768]{1,0:T(8,128)(2,1)S(1)} %bitcast.21, bf16[64,768]{1,0:T(8,128)(2,1)S(1)} %fusion.2.own_ref), custom_call_target="tpu_custom_call" | custom-call | tf_op jit(solution)/shard_map/pallas_call | solution.py:54
  (1 shorter events, 0.0 us)
Async XLA Ops:
  30.4 0.9 %copy-start = (f32[1,64,768]{2,1,0:T(8,128)S(1)}, f32[1,64,768]{2,1,0:T(8,128)}, u32[]{:S(2)}) copy-start(f32[1,64,768]{2,1,0:T(8,128)} %param.3) | copy-start | bytes 589828
  33.4 26.2 %all-to-all-start.1 = ((bf16[16,64,768]{2,1,0:T(8,128)(2,1)}), bf16[16,64,768]{2,1,0:T(8,128)(2,1)S(1)}, u32[]{:S(2)}, u32[]{:S(2)}) async-start(bf16[16,64,768]{2,1,0:T(8,128)(2,1)} %broadcast_in_dim.13), calls=%async_computation.1 | async-start | bytes 3145728 | tf_op jit(solution)/shard_map/all_to_all | solution.py:71

commit v2 on v1

v2 whole, which is shorter than its diff:
```python
import functools
import math

import jax
import jax.numpy as jnp
from jax import lax
from jax.experimental import pallas as pl
from jax.experimental.pallas import tpu as pltpu
from jax.sharding import PartitionSpec as P

D = 1024
R = 768
N_EXPERT = 16
ROWS = D // N_EXPERT
SIDE = 4
TILE = 256


rate = 0.95
eps = 1e-07
coef_a = 3.4445
coef_b = -4.775
coef_c = 2.0315
share = rate * rate / (1 + rate)
f32 = jnp.float32
bf16 = jnp.bfloat16
VMEM = pl.BlockSpec(memory_space=pltpu.VMEM)
SMALL = pltpu.CompilerParams(vmem_limit_bytes=8 * 2**20)


def dot(lhs, rhs, side=1):
    return lax.dot_general(lhs, rhs, (((side,), (0,)), ((), ())), preferred_element_type=f32)


def mirror(target, column, value):
    cols = slice(column * TILE, (column + 1) * TILE)
    target[: (column + 1) * TILE, cols] = value
    for row in range(column):
        target[cols, row * TILE : (row + 1) * TILE] = jnp.transpose(value[row * TILE : (row + 1) * TILE, :])


def symmetric(target, lhs, rhs, linear, scale, factor):
    for column in range(R // TILE):
        cols, depth = slice(column * TILE, (column + 1) * TILE), (column + 1) * TILE
        product = dot(lhs[:depth, :], rhs[:, cols])
        mirror(target, column, (scale * linear[:depth, cols].astype(f32) + factor * product).astype(bf16))


def newton_schulz(whole_ref, out_ref, wide, gram, poly, half):
    squares = jnp.zeros((1, 1), f32)
    diagonal = lax.broadcasted_iota(jnp.int32, (TILE, TILE), 0) == lax.broadcasted_iota(jnp.int32, (TILE, TILE), 1)
    for column in range(R // TILE):
        cols, depth = slice(column * TILE, (column + 1) * TILE), (column + 1) * TILE
        wide[:depth, cols] = dot(whole_ref[:, :depth], whole_ref[:, cols], side=0)
        squares += jnp.sum(jnp.where(diagonal, wide[cols, cols], 0.0))
    inverse = 1.0 / (jnp.sqrt(squares) + eps / (1 + rate))
    for column in range(R // TILE):
        cols, depth = slice(column * TILE, (column + 1) * TILE), (column + 1) * TILE
        mirror(gram, column, (wide[:depth, cols] * inverse * inverse).astype(bf16))

    symmetric(poly, gram, gram, gram, coef_b, coef_c)
    symmetric(half, gram, poly, gram, coef_a, 1.0)
    expert, start = lax.axis_index("expert"), place() * ROWS
    start += jnp.where(lax.axis_index("dp") % 2 == 0, expert % SIDE, expert // SIDE) * SIDE * ROWS
    rows = whole_ref[pl.ds(pl.multiple_of(start, ROWS), ROWS), :]
    rows = (inverse * (coef_a * rows.astype(f32) + dot(rows, poly[...]))).astype(bf16)
    symmetric(gram, half, poly, half, coef_a, 1.0)
    symmetric(poly, gram, gram, gram, coef_b, coef_c)

    def step(value):
        return (coef_a * value.astype(f32) + dot(value, poly[...])).astype(bf16)

    def last_gram(value):
        return dot(step(step(value)), gram[...])

    rows = step(rows)
    once = last_gram(rows)
    twice = last_gram(once.astype(bf16))
    rows = (coef_a * rows.astype(f32) + coef_b * once + coef_c * twice).astype(bf16)
    factor = 0.2 * math.sqrt(max(D, R))
    out_ref[...] = (factor * rows.astype(f32)).astype(bf16)


def orthogonalize(whole):
    return pl.pallas_call(
        newton_schulz,
        out_shape=jax.ShapeDtypeStruct((ROWS, R), bf16),
        in_specs=[VMEM],
        out_specs=VMEM,
        scratch_shapes=[
            pltpu.VMEM((R, R), f32),
            pltpu.VMEM((R, R), bf16),
            pltpu.VMEM((R, R), bf16),
            pltpu.VMEM((R, R), bf16),
        ],
        compiler_params=pltpu.CompilerParams(vmem_limit_bytes=20 * 2**20),
    )(whole)


def place():
    expert = lax.axis_index("expert")
    return jnp.where(lax.axis_index("dp") % 2 == 0, expert // SIDE, expert % SIDE)


def order(grads):
    along_x = lax.axis_index("dp") % 2 == 0
    tiles = grads.reshape(SIDE, SIDE, ROWS, R)
    return lax.cond(along_x, lambda t: jnp.swapaxes(t, 0, 1), lambda t: t, tiles)


def partial_kernel(terms_ref, momentum_ref, sent_ref, own_ref):
    mine = place()
    for sub in range(SIDE):
        total = sum(terms_ref[peer, sub].astype(f32) for peer in range(SIDE))
        weight = jnp.where(mine == sub, share, 0.0).astype(f32)
        sent = (total + weight * momentum_ref[...]).astype(bf16)
        for peer in range(SIDE):
            sent_ref[peer, sub] = sent
    own_ref[...] = sum(terms_ref[peer, mine].astype(f32) for peer in range(SIDE))


def partial_sums(terms, momentum):
    return pl.pallas_call(
        partial_kernel,
        out_shape=(jax.ShapeDtypeStruct((SIDE, SIDE, ROWS, R), bf16), jax.ShapeDtypeStruct((ROWS, R), f32)),
        in_specs=[VMEM, VMEM],
        out_specs=(VMEM, VMEM),
        compiler_params=SMALL,
    )(terms, momentum)


def blend_kernel(got_ref, own_ref, sent_ref, total_ref):
    mine = place()
    for sub in range(SIDE):
        blend = sum(got_ref[peer, sub].astype(f32) for peer in range(SIDE)).astype(bf16)
        for peer in range(SIDE):
            sent_ref[peer, sub] = blend
    total_ref[...] = own_ref[...] + sum(
        jnp.where(mine == peer, 0.0, 1.0).astype(f32) * got_ref[peer, mine].astype(f32) for peer in range(SIDE)
    )


def blends(got, own):
    return pl.pallas_call(
        blend_kernel,
        out_shape=(jax.ShapeDtypeStruct((SIDE, SIDE, ROWS, R), bf16), jax.ShapeDtypeStruct((ROWS, R), f32)),
        in_specs=[VMEM, VMEM],
        out_specs=(VMEM, VMEM),
        compiler_params=SMALL,
    )(got, own)


def exchange(blocks, groups):
    return lax.all_to_all(blocks, ("dp", "expert"), 0, 0, tiled=True, axis_index_groups=groups)


def lines(count, first):
    groups = []
    for dp in range(count):
        for fixed in range(SIDE):
            along_x = [fixed * SIDE + moving for moving in range(SIDE)]
            along_y = [moving * SIDE + fixed for moving in range(SIDE)]
            groups.append([dp * N_EXPERT + e for e in (along_x if dp % 2 == first else along_y)])
    return groups


def shards(count, grads, momentum):
    first, second = lines(count, 0), lines(count, 1)
    terms = exchange(order(grads), first)
    sent, own = partial_sums(terms, momentum[0])
    sent, total = blends(exchange(sent, second), own)
    whole = exchange(sent, first).reshape(D, R)
    new_momentum = rate * momentum[0] + total
    return (orthogonalize(whole)[None], new_momentum[None])


def solution(mesh):
    return jax.shard_map(
        functools.partial(shards, mesh.shape["dp"]),
        mesh=mesh,
        in_specs=(P("expert", "dp", None, None), P("dp", "expert", None)),
        out_specs=(P("dp", "expert", None), P("dp", "expert", None)),
        check_vma=False,
    )
```

time: 70.2 us -> 79.3 us (1.13)
  the two profiles are of different devices: /device:TPU:992 before, /device:TPU:2 now
where the time goes in v2:
time: 79.3 us; the launch traced here: 79.1 us
  blocking collectives  50.7 us (64%)
  waiting for transfers between devices  11.5 us (15%)
  Pallas kernels  8.85 us (11%)
  starting transfers between devices  5 us (6%)
  local copies, waits for them, and re-layouts  1.53 us (2%)
    all_to_all x2, blocking collectives, exchange(): lax.all_to_all(blocks, ('dp', 'expert'), 0, 0, tiled=True, axis_index_gro...  50.7 us
    all_to_all x1, waiting for transfers between devices, exchange(): lax.all_to_all(blocks, ('dp', 'expert'), 0, 0, tiled=True, axis_index_gro...  11.5 us
    pallas_call x1, Pallas kernels, orthogonalize(): pl.pallas_call(newton_schulz, out_shape=jax.ShapeDtypeStruct((ROWS, R), b...  7.21 us
    all_to_all x1, starting transfers between devices, exchange(): lax.all_to_all(blocks, ('dp', 'expert'), 0, 0, tiled=True, axis_index_gro...  5 us
  transfers between devices with their start and end apart: 1, of which 1 were waited for; matrix products, arithmetic and copies ran while one was open for 1% of the time, Pallas kernels for 0%

profile of v2, /device:TPU:2, one launch (start us, length us, event | category | flops | bytes accessed | tf_op | source)
XLA Modules:
  0.0 79.1 jit_solution(3202006266610730944)
XLA Ops:
  0.6 1.4 %conditional.1 = (bf16[4,4,64,768]{3,2,0,1:T(8,128)(2,1)S(1)}) conditional(s32[]{:T(128)} %convert_element_type.3, bf16[4,4,64,768]{3,2,1,0:T(8,128)(2,1)} %bitcast.10, bf16[4,4,64,768]{3,2,1,0:T(8,128)(2,1)} %bitcast.11), branch_computations={%region_0.1_spmd, %region_1.2_spmd} | conditional | bytes 3145736 | solution.py:108
  0.7 1.4 %copy.7 = bf16[4,4,64,768]{3,2,0,1:T(8,128)(2,1)S(1)} copy(bf16[4,4,64,768]{3,2,0,1:T(8,128)(2,1)} %bitcast.12) | data formatting | bytes 3145728 | tf_op jit(solution)/shard_map/cond
  2.1 0.1 copy.5
  2.2 0.0 copy-start
  2.2 31.8 %all_to_all.15.terms_ref = bf16[4,4,64,768]{3,2,1,0:T(8,128)(2,1)S(1)} all-to-all(bf16[4,4,64,768]{3,2,1,0:T(8,128)(2,1)S(1)} %copy.5), channel_id=1, replica_groups={{0,1,2,3},{4,5,6,7},{8,9,10,11},{12,13,14,15},{16,20,24,28},{17,21,25,2..., dimensions={0} | all-to-all | bytes 3145728 | tf_op jit(solution)/shard_map/all_to_all | solution.py:154
  34.0 0.0 copy-done
  34.0 0.3 shard_map.41
  34.3 18.9 %all_to_all.16.got_ref = bf16[4,4,64,768]{3,2,1,0:T(8,128)(2,1)S(1)} all-to-all(bf16[4,4,64,768]{3,2,1,0:T(8,128)(2,1)S(1)} %get-tuple-element.11), channel_id=1, replica_groups={{0,4,8,12},{1,5,9,13},{2,6,10,14},{3,7,11,15},{16,17,18,19},{20,21,22,2..., dimensions={0} | all-to-all | bytes 3145728 | tf_op jit(solution)/shard_map/all_to_all | solution.py:154
  53.2 1.4 %shard_map.42 = (bf16[4,4,64,768]{3,2,1,0:T(8,128)(2,1)}, f32[64,768]{1,0:T(8,128)S(1)}) custom-call(bf16[4,4,64,768]{3,2,1,0:T(8,128)(2,1)S(1)} %all_to_all.16.got_ref, f32[64,768]{1,0:T(8,128)S(1)} %get-tuple-element.12.own_ref), custom_call_target="tpu_custom_call" | custom-call | tf_op jit(solution)/shard_map/pallas_call | solution.py:144
  54.6 5.0 %all-to-all-start.2 = ((bf16[4,4,64,768]{3,2,1,0:T(8,128)(2,1)}), bf16[4,4,64,768]{3,2,1,0:T(8,128)(2,1)S(1)}, u32[]{:S(2)}, u32[]{:S(2)}) async-start(bf16[4,4,64,768]{3,2,1,0:T(8,128)(2,1)} %get-tuple-element.13), calls=%async_computation.2 | async-start | bytes 3145728 | tf_op jit(solution)/shard_map/all_to_all | solution.py:154
  59.6 0.7 add_bitcast_fusion
  60.3 11.5 %all-to-all-done.2 = bf16[4,4,64,768]{3,2,1,0:T(8,128)(2,1)S(1)} async-done(((bf16[4,4,64,768]{3,2,1,0:T(8,128)(2,1)}), bf16[4,4,64,768]{3,2,1,0:T(8,128)(2,1)S(1)}, u32[]{:S(2)}, u32[]{:S(2)}) %all-to-all-start.2) | async-done | bytes 1572896 | tf_op jit(solution)/shard_map/all_to_all | solution.py:154
  71.8 7.2 %shard_map.43 = bf16[64,768]{1,0:T(8,128)(2,1)} custom-call(bf16[1024,768]{1,0:T(8,128)(2,1)S(1)} %bitcast.8), custom_call_target="tpu_custom_call" | custom-call | tf_op jit(solution)/shard_map/pallas_call | solution.py:85
Async XLA Ops:
  2.2 31.8 %copy-start = (f32[1,64,768]{2,1,0:T(8,128)S(1)}, f32[1,64,768]{2,1,0:T(8,128)}, u32[]{:S(2)}) copy-start(f32[1,64,768]{2,1,0:T(8,128)} %param.5) | copy-start | bytes 589828
  54.6 17.2 %all-to-all-start.2 = ((bf16[4,4,64,768]{3,2,1,0:T(8,128)(2,1)}), bf16[4,4,64,768]{3,2,1,0:T(8,128)(2,1)S(1)}, u32[]{:S(2)}, u32[]{:S(2)}) async-start(bf16[4,4,64,768]{3,2,1,0:T(8,128)(2,1)} %get-tuple-element.13), calls=%async_computation.2 | async-start | bytes 3145728 | tf_op jit(solution)/shard_map/all_to_all | solution.py:154

commit v3 on v2

v3 whole, which is shorter than its diff:
```python
import math

import jax
import jax.numpy as jnp
from jax import lax
from jax.experimental import pallas as pl
from jax.experimental.pallas import tpu as pltpu
from jax.sharding import PartitionSpec as P

D = 1024
R = 768
N_EXPERT = 16
ROWS = D // N_EXPERT
TILE = 256


rate = 0.95
eps = 1e-07
coef_a = 3.4445
coef_b = -4.775
coef_c = 2.0315
f32 = jnp.float32
bf16 = jnp.bfloat16
VMEM = pl.BlockSpec(memory_space=pltpu.VMEM)
SMALL = pltpu.CompilerParams(vmem_limit_bytes=8 * 2**20)


def dot(lhs, rhs, side=1):
    return lax.dot_general(lhs, rhs, (((side,), (0,)), ((), ())), preferred_element_type=f32)


def mirror(target, column, value):
    cols = slice(column * TILE, (column + 1) * TILE)
    target[: (column + 1) * TILE, cols] = value
    for row in range(column):
        target[cols, row * TILE : (row + 1) * TILE] = jnp.transpose(value[row * TILE : (row + 1) * TILE, :])


def symmetric(target, lhs, rhs, linear, scale, factor):
    for column in range(R // TILE):
        cols, depth = slice(column * TILE, (column + 1) * TILE), (column + 1) * TILE
        product = dot(lhs[:depth, :], rhs[:, cols])
        mirror(target, column, (scale * linear[:depth, cols].astype(f32) + factor * product).astype(bf16))


def newton_schulz(whole_ref, total_ref, momentum_ref, out_ref, new_ref, wide, gram, poly, half, fresh, sem):
    fresh[...] = rate * momentum_ref[...] + total_ref[...]
    leave = pltpu.make_async_copy(fresh, new_ref, sem)
    leave.start()

    squares = jnp.zeros((1, 1), f32)
    diagonal = lax.broadcasted_iota(jnp.int32, (TILE, TILE), 0) == lax.broadcasted_iota(jnp.int32, (TILE, TILE), 1)
    for column in range(R // TILE):
        cols, depth = slice(column * TILE, (column + 1) * TILE), (column + 1) * TILE
        wide[:depth, cols] = dot(whole_ref[:, :depth], whole_ref[:, cols], side=0)
        squares += jnp.sum(jnp.where(diagonal, wide[cols, cols], 0.0))
    inverse = 1.0 / (jnp.sqrt(squares) + eps)
    for column in range(R // TILE):
        cols, depth = slice(column * TILE, (column + 1) * TILE), (column + 1) * TILE
        mirror(gram, column, (wide[:depth, cols] * inverse * inverse).astype(bf16))

    symmetric(poly, gram, gram, gram, coef_b, coef_c)
    symmetric(half, gram, poly, gram, coef_a, 1.0)
    start = pl.multiple_of(lax.axis_index("expert") * ROWS, ROWS)
    rows = whole_ref[pl.ds(start, ROWS), :]
    rows = (inverse * (coef_a * rows.astype(f32) + dot(rows, poly[...]))).astype(bf16)
    symmetric(gram, half, poly, half, coef_a, 1.0)
    symmetric(poly, gram, gram, gram, coef_b, coef_c)

    def step(value):
        return (coef_a * value.astype(f32) + dot(value, poly[...])).astype(bf16)

    def last_gram(value):
        return dot(step(step(value)), gram[...])

    rows = step(rows)
    once = last_gram(rows)
    twice = last_gram(once.astype(bf16))
    rows = (coef_a * rows.astype(f32) + coef_b * once + coef_c * twice).astype(bf16)
    factor = 0.2 * math.sqrt(max(D, R))
    out_ref[...] = (factor * rows.astype(f32)).astype(bf16)
    leave.wait()


def orthogonalize(whole, total, momentum):
    return pl.pallas_call(
        newton_schulz,
        out_shape=(jax.ShapeDtypeStruct((ROWS, R), bf16), jax.ShapeDtypeStruct((ROWS, R), f32)),
        in_specs=[VMEM, VMEM, VMEM],
        out_specs=(VMEM, pl.BlockSpec(memory_space=pl.ANY)),
        scratch_shapes=[
            pltpu.VMEM((R, R), f32),
            pltpu.VMEM((R, R), bf16),
            pltpu.VMEM((R, R), bf16),
            pltpu.VMEM((R, R), bf16),
            pltpu.VMEM((ROWS, R), f32),
            pltpu.SemaphoreType.DMA,
        ],
        compiler_params=pltpu.CompilerParams(vmem_limit_bytes=20 * 2**20),
    )(whole, total, momentum)


def blend_kernel(terms_ref, momentum_ref, sent_ref, total_ref):
    total = sum(terms_ref[peer].astype(f32) for peer in range(N_EXPERT))
    total_ref[...] = total
    blend = (total + rate * (rate * momentum_ref[...] + total)).astype(bf16)
    for peer in range(N_EXPERT):
        sent_ref[peer] = blend


def blends(terms, momentum):
    return pl.pallas_call(
        blend_kernel,
        out_shape=(jax.ShapeDtypeStruct((N_EXPERT, ROWS, R), bf16), jax.ShapeDtypeStruct((ROWS, R), f32)),
        in_specs=[VMEM, VMEM],
        out_specs=(VMEM, VMEM),
        compiler_params=SMALL,
    )(terms, momentum)


def exchange(blocks):
    return lax.all_to_all(blocks, "expert", 0, 0, tiled=True)


def shards(grads, momentum):
    sent, total = blends(exchange(grads.reshape(N_EXPERT, ROWS, R)), momentum[0])
    update, new_momentum = orthogonalize(exchange(sent).reshape(D, R), total, momentum[0])
    return (update[None], new_momentum[None])


def solution(mesh):
    return jax.shard_map(
        shards,
        mesh=mesh,
        in_specs=(P("expert", "dp", None, None), P("dp", "expert", None)),
        out_specs=(P("dp", "expert", None), P("dp", "expert", None)),
        check_vma=False,
    )
```

time: 79.3 us -> 63.9 us (0.81)
  the two profiles are of different devices: /device:TPU:2 before, /device:TPU:992 now
where the time goes in v3:
time: 63.9 us; the launch traced here: 63.7 us
  blocking collectives  55 us (86%)
  Pallas kernels  8.11 us (13%)
  between operations  0.64 us (1%)
    all_to_all x2, blocking collectives, exchange(): return lax.all_to_all(blocks, 'expert', 0, 0, tiled=True)  55 us
    pallas_call x1, Pallas kernels, orthogonalize(): pl.pallas_call(newton_schulz, out_shape=(jax.ShapeDtypeStruct((ROWS, R),...  7.82 us

profile of v3, /device:TPU:992, one launch (start us, length us, event | category | flops | bytes accessed | tf_op | source)
XLA Modules:
  0.0 63.7 jit_solution(1228167810691821258)
XLA Ops:
  0.6 0.0 copy-start
  0.6 29.9 %all_to_all.10.terms_ref = bf16[16,64,768]{2,1,0:T(8,128)(2,1)S(1)} all-to-all(bf16[16,64,768]{2,1,0:T(8,128)(2,1)} %bitcast.8), channel_id=1, replica_groups=mesh['dp'=64,'expert'=16] {'expert'}, dimensions={0} | all-to-all | bytes 3145728 | tf_op jit(solution)/shard_map/all_to_all | solution.py:122
  30.6 0.0 copy-done
  30.6 0.3 shard_map.41
  30.9 25.0 %all_to_all.11 = bf16[16,64,768]{2,1,0:T(8,128)(2,1)S(1)} all-to-all(bf16[16,64,768]{2,1,0:T(8,128)(2,1)S(1)} %get-tuple-element.6), channel_id=1, replica_groups=mesh['dp'=64,'expert'=16] {'expert'}, dimensions={0} | all-to-all | bytes 3145728 | tf_op jit(solution)/shard_map/all_to_all | solution.py:122
  55.9 7.8 %shard_map.42 = (bf16[64,768]{1,0:T(8,128)(2,1)}, f32[64,768]{1,0:T(8,128)}) custom-call(bf16[1024,768]{1,0:T(8,128)(2,1)S(1)} %bitcast.5, f32[64,768]{1,0:T(8,128)S(1)} %get-tuple-element.7.total_ref, f32[64,768]{1,0:T(8,128)S(1)} %bitcast.7), custom_call_target="tpu_custom_call" | custom-call | tf_op jit(solution)/shard_map/pallas_call | solution.py:86
Async XLA Ops:
  0.6 30.0 %copy-start = (f32[1,64,768]{2,1,0:T(8,128)S(1)}, f32[1,64,768]{2,1,0:T(8,128)}, u32[]{:S(2)}) copy-start(f32[1,64,768]{2,1,0:T(8,128)} %param.3) | copy-start | bytes 589828

commit v4 on v3

--- a/solution.py
+++ b/solution.py
@@ -43,21 +43,19 @@
         mirror(target, column, (scale * linear[:depth, cols].astype(f32) + factor * product).astype(bf16))
 
 
-def newton_schulz(whole_ref, total_ref, momentum_ref, out_ref, new_ref, wide, gram, poly, half, fresh, sem):
-    fresh[...] = rate * momentum_ref[...] + total_ref[...]
-    leave = pltpu.make_async_copy(fresh, new_ref, sem)
+def newton_schulz(whole_ref, fresh_ref, out_ref, new_ref, gram, poly, half, sem):
+    leave = pltpu.make_async_copy(fresh_ref, new_ref, sem)
     leave.start()
 
-    squares = jnp.zeros((1, 1), f32)
-    diagonal = lax.broadcasted_iota(jnp.int32, (TILE, TILE), 0) == lax.broadcasted_iota(jnp.int32, (TILE, TILE), 1)
+    squares = jnp.zeros((ROWS, R), f32)
+    for block in range(N_EXPERT):
+        part = whole_ref[block * ROWS : (block + 1) * ROWS, :].astype(f32)
+        squares += part * part
+    inverse = 1.0 / (jnp.sqrt(jnp.full((1, 1), jnp.sum(squares), f32)) + eps)
     for column in range(R // TILE):
         cols, depth = slice(column * TILE, (column + 1) * TILE), (column + 1) * TILE
-        wide[:depth, cols] = dot(whole_ref[:, :depth], whole_ref[:, cols], side=0)
-        squares += jnp.sum(jnp.where(diagonal, wide[cols, cols], 0.0))
-    inverse = 1.0 / (jnp.sqrt(squares) + eps)
-    for column in range(R // TILE):
-        cols, depth = slice(column * TILE, (column + 1) * TILE), (column + 1) * TILE
-        mirror(gram, column, (wide[:depth, cols] * inverse * inverse).astype(bf16))
+        product = dot(whole_ref[:, :depth], whole_ref[:, cols], side=0)
+        mirror(gram, column, (product * (inverse * inverse)).astype(bf16))
 
     symmetric(poly, gram, gram, gram, coef_b, coef_c)
     symmetric(half, gram, poly, gram, coef_a, 1.0)
@@ -82,28 +80,27 @@
     leave.wait()
 
 
-def orthogonalize(whole, total, momentum):
+def orthogonalize(whole, fresh):
     return pl.pallas_call(
         newton_schulz,
         out_shape=(jax.ShapeDtypeStruct((ROWS, R), bf16), jax.ShapeDtypeStruct((ROWS, R), f32)),
-        in_specs=[VMEM, VMEM, VMEM],
+        in_specs=[VMEM, VMEM],
         out_specs=(VMEM, pl.BlockSpec(memory_space=pl.ANY)),
         scratch_shapes=[
-            pltpu.VMEM((R, R), f32),
             pltpu.VMEM((R, R), bf16),
             pltpu.VMEM((R, R), bf16),
             pltpu.VMEM((R, R), bf16),
-            pltpu.VMEM((ROWS, R), f32),
             pltpu.SemaphoreType.DMA,
         ],
         compiler_params=pltpu.CompilerParams(vmem_limit_bytes=20 * 2**20),
-    )(whole, total, momentum)
+    )(whole, fresh)
 
 
-def blend_kernel(terms_ref, momentum_ref, sent_ref, total_ref):
+def blend_kernel(terms_ref, momentum_ref, sent_ref, fresh_ref):
     total = sum(terms_ref[peer].astype(f32) for peer in range(N_EXPERT))
-    total_ref[...] = total
-    blend = (total + rate * (rate * momentum_ref[...] + total)).astype(bf16)
+    fresh = rate * momentum_ref[...] + total
+    fresh_ref[...] = fresh
+    blend = (total + rate * fresh).astype(bf16)
     for peer in range(N_EXPERT):
         sent_ref[peer] = blend
 
@@ -123,8 +120,8 @@
 
 
 def shards(grads, momentum):
-    sent, total = blends(exchange(grads.reshape(N_EXPERT, ROWS, R)), momentum[0])
-    update, new_momentum = orthogonalize(exchange(sent).reshape(D, R), total, momentum[0])
+    sent, fresh = blends(exchange(grads.reshape(N_EXPERT, ROWS, R)), momentum[0])
+    update, new_momentum = orthogonalize(exchange(sent).reshape(D, R), fresh)
     return (update[None], new_momentum[None])
 
 

time: 63.9 us -> 62.8 us (0.983)
  Pallas kernels: 8.11 us -> 6.98 us
    pallas_call x1, Pallas kernels: 7.82 us -> 6.69 us  [orthogonalize(): pl.pallas_call(newton_schulz, out_shape=(jax.ShapeDtypeStruct((ROWS, R),...]
where the time goes in v4:
time: 62.8 us; the launch traced here: 62.6 us
  blocking collectives  55 us (88%)
  Pallas kernels  6.98 us (11%)
  between operations  0.64 us (1%)
    all_to_all x2, blocking collectives, exchange(): return lax.all_to_all(blocks, 'expert', 0, 0, tiled=True)  55 us
    pallas_call x1, Pallas kernels, orthogonalize(): pl.pallas_call(newton_schulz, out_shape=(jax.ShapeDtypeStruct((ROWS, R),...  6.69 us

profile of v4, /device:TPU:992, one launch (start us, length us, event | category | flops | bytes accessed | tf_op | source)
XLA Modules:
  0.0 62.6 jit_solution(1747214318954118397)
XLA Ops:
  0.6 0.0 copy-start
  0.6 29.9 %all_to_all.10.terms_ref = bf16[16,64,768]{2,1,0:T(8,128)(2,1)S(1)} all-to-all(bf16[16,64,768]{2,1,0:T(8,128)(2,1)} %bitcast.7), channel_id=1, replica_groups=mesh['dp'=64,'expert'=16] {'expert'}, dimensions={0} | all-to-all | bytes 3145728 | tf_op jit(solution)/shard_map/all_to_all | solution.py:119
  30.6 0.0 copy-done
  30.6 0.3 shard_map.41
  30.9 25.0 %all_to_all.11 = bf16[16,64,768]{2,1,0:T(8,128)(2,1)S(1)} all-to-all(bf16[16,64,768]{2,1,0:T(8,128)(2,1)S(1)} %get-tuple-element.6), channel_id=1, replica_groups=mesh['dp'=64,'expert'=16] {'expert'}, dimensions={0} | all-to-all | bytes 3145728 | tf_op jit(solution)/shard_map/all_to_all | solution.py:119
  55.9 6.7 %shard_map.42 = (bf16[64,768]{1,0:T(8,128)(2,1)}, f32[64,768]{1,0:T(8,128)}) custom-call(bf16[1024,768]{1,0:T(8,128)(2,1)S(1)} %bitcast.5, f32[64,768]{1,0:T(8,128)S(1)} %get-tuple-element.7.fresh_ref), custom_call_target="tpu_custom_call" | custom-call | tf_op jit(solution)/shard_map/pallas_call | solution.py:84
Async XLA Ops:
  0.6 30.0 %copy-start = (f32[1,64,768]{2,1,0:T(8,128)S(1)}, f32[1,64,768]{2,1,0:T(8,128)}, u32[]{:S(2)}) copy-start(f32[1,64,768]{2,1,0:T(8,128)} %param.3) | copy-start | bytes 589828

commit v5 on v4

--- a/solution.py
+++ b/solution.py
@@ -1,3 +1,4 @@
+import functools
 import math
 
 import jax
@@ -59,7 +60,9 @@
 
     symmetric(poly, gram, gram, gram, coef_b, coef_c)
     symmetric(half, gram, poly, gram, coef_a, 1.0)
-    start = pl.multiple_of(lax.axis_index("expert") * ROWS, ROWS)
+    expert = lax.axis_index("expert")
+    position = jnp.where(lax.axis_index("dp") % 2 == 0, expert, N_EXPERT - 1 - expert)
+    start = pl.multiple_of(position * ROWS, ROWS)
     rows = whole_ref[pl.ds(start, ROWS), :]
     rows = (inverse * (coef_a * rows.astype(f32) + dot(rows, poly[...]))).astype(bf16)
     symmetric(gram, half, poly, half, coef_a, 1.0)
@@ -119,15 +122,21 @@
     return lax.all_to_all(blocks, "expert", 0, 0, tiled=True)
 
 
-def shards(grads, momentum):
+def spread(blocks, count):
+    order = range(N_EXPERT)
+    groups = [[dp * N_EXPERT + e for e in (order if dp % 2 == 0 else order[::-1])] for dp in range(count)]
+    return lax.all_to_all(blocks, ("dp", "expert"), 0, 0, tiled=True, axis_index_groups=groups)
+
+
+def shards(count, grads, momentum):
     sent, fresh = blends(exchange(grads.reshape(N_EXPERT, ROWS, R)), momentum[0])
-    update, new_momentum = orthogonalize(exchange(sent).reshape(D, R), fresh)
+    update, new_momentum = orthogonalize(spread(sent, count).reshape(D, R), fresh)
     return (update[None], new_momentum[None])
 
 
 def solution(mesh):
     return jax.shard_map(
-        shards,
+        functools.partial(shards, mesh.shape["dp"]),
         mesh=mesh,
         in_specs=(P("expert", "dp", None, None), P("dp", "expert", None)),
         out_specs=(P("dp", "expert", None), P("dp", "expert", None)),

time: 62.8 us -> 61.7 us (0.982)
  blocking collectives: 55 us -> 53.9 us
    all_to_all x2 -> x1, blocking collectives: 55 us -> 29.9 us  [exchange(): return lax.all_to_all(blocks, 'expert', 0, 0, tiled=True)]
    all_to_all x0 -> x1, blocking collectives: none -> 23.9 us  [spread(): lax.all_to_all(blocks, ('dp', 'expert'), 0, 0, tiled=True, axis_index_gro...]
where the time goes in v5:
time: 61.7 us; the launch traced here: 61.5 us
  blocking collectives  53.9 us (87%)
  Pallas kernels  6.98 us (11%)
  between operations  0.64 us (1%)
    all_to_all x1, blocking collectives, exchange(): return lax.all_to_all(blocks, 'expert', 0, 0, tiled=True)  29.9 us
    all_to_all x1, blocking collectives, spread(): lax.all_to_all(blocks, ('dp', 'expert'), 0, 0, tiled=True, axis_index_gro...  23.9 us
    pallas_call x1, Pallas kernels, orthogonalize(): pl.pallas_call(newton_schulz, out_shape=(jax.ShapeDtypeStruct((ROWS, R),...  6.69 us

profile of v5, /device:TPU:992, one launch (start us, length us, event | category | flops | bytes accessed | tf_op | source)
XLA Modules:
  0.0 61.5 jit_solution(3744338775526621354)
XLA Ops:
  0.6 0.0 copy-start
  0.6 29.9 %all_to_all.10.terms_ref = bf16[16,64,768]{2,1,0:T(8,128)(2,1)S(1)} all-to-all(bf16[16,64,768]{2,1,0:T(8,128)(2,1)} %bitcast.7), channel_id=1, replica_groups=mesh['dp'=64,'expert'=16] {'expert'}, dimensions={0} | all-to-all | bytes 3145728 | tf_op jit(solution)/shard_map/all_to_all | solution.py:122
  30.6 0.0 copy-done
  30.6 0.3 shard_map.41
  30.9 23.9 %all_to_all.11 = bf16[16,64,768]{2,1,0:T(8,128)(2,1)S(1)} all-to-all(bf16[16,64,768]{2,1,0:T(8,128)(2,1)S(1)} %get-tuple-element.6), channel_id=1, replica_groups={{0,1,2,3,4,5,6,7,8,9,10,11,12,13,14,15},{31,30,29,28,27,26,25,24,23,22,..., dimensions={0} | all-to-all | bytes 3145728 | tf_op jit(solution)/shard_map/all_to_all | solution.py:128
  54.8 6.7 %shard_map.42 = (bf16[64,768]{1,0:T(8,128)(2,1)}, f32[64,768]{1,0:T(8,128)}) custom-call(bf16[1024,768]{1,0:T(8,128)(2,1)S(1)} %bitcast.5, f32[64,768]{1,0:T(8,128)S(1)} %get-tuple-element.7.fresh_ref), custom_call_target="tpu_custom_call" | custom-call | tf_op jit(solution)/shard_map/pallas_call | solution.py:87
Async XLA Ops:
  0.6 30.0 %copy-start = (f32[1,64,768]{2,1,0:T(8,128)S(1)}, f32[1,64,768]{2,1,0:T(8,128)}, u32[]{:S(2)}) copy-start(f32[1,64,768]{2,1,0:T(8,128)} %param.3) | copy-start | bytes 589828
